TPU v7x, 256 devices: a whole 4x4x8 slice. The times are simulated.
256 devices in a mesh: bins: 64 (over x, z, core), panel: 4 (over y).
Axes of the slice: x: 4, y: 4, z: 8, core: 2. Of those that a mesh axis runs over, the one named last changes fastest.
Arguments:
- records: bfloat16 [16, 4096, 9216], P('panel', 'bins'), may hold values from -6 to 6
- valid: int32 [16, 4096], P('panel', 'bins'), may hold values 0 or 1
- offsets: int32 [16, 16], replicated, may hold values from 0 to 8192, as said below
Outputs:
- csd: bfloat16 [64, 4096, 4096], P('bins', 'panel')
Inputs may be any that keep to these rules, and one draw needn't show every extreme that they name: offsets[w, s] lies between s * 512 and (s + 1) * 512.
All inputs are finite; a program needn't handle non-finite values. No bound on the sum of `valid` on one device may be relied on, other than what follows from the above.
Results may differ from a plain program's by a relative error of at most 0.007.
Values may be sent and summed in bfloat16 or wider, within the bound.
A program may use at most 64 MiB of HBM per device.

v0:
```python
import jax
import jax.numpy as jnp
from jax import lax
from jax.sharding import PartitionSpec as P

SEGLEN = 1024
SEG = 16
BAND0 = 64
F_DEV = 1


def weight_values(pos, freq, part, seglen):
    posf = pos.astype(jnp.float32)
    hann = 0.5 - 0.5 * jnp.cos(2.0 * jnp.pi * posf / seglen)
    taper = hann / jnp.sqrt(jnp.float32(0.375 * seglen))
    phase = (freq * pos % seglen).astype(jnp.float32) * (2.0 * jnp.pi / seglen)
    trig = jnp.where(part == 0, jnp.cos(phase), -jnp.sin(phase))
    return taper * trig


def make_weight(nbins):
    rows = jnp.arange(2 * nbins, dtype=jnp.int32)
    part = (rows // nbins)[:, None]
    freq = (BAND0 + rows % nbins)[:, None]
    pos = jnp.arange(SEGLEN, dtype=jnp.int32)[None, :]
    return weight_values(pos, freq, part, SEGLEN).astype(jnp.bfloat16)


def contract(block, row_start, row_count):
    halves = block.reshape(block.shape[0] // 2, 2, block.shape[1], block.shape[2])
    rows = lax.dynamic_slice_in_dim(halves, row_start, row_count, 3)
    real_part = rows[:, 0].astype(jnp.float32)
    imag_part = rows[:, 1].astype(jnp.float32)
    left = jnp.stack([real_part + imag_part, imag_part - real_part], axis=1).astype(jnp.bfloat16)
    return jnp.einsum("kpfr,kpfc->frc", left, halves, preferred_element_type=jnp.float32)


def body(records, valid, offsets):
    wins_local = records.shape[0]
    chan_local = records.shape[1]
    panels = lax.axis_size("panel")
    nbins = F_DEV * lax.axis_size("bins")
    first = lax.axis_index("panel") * wins_local
    my_offsets = lax.dynamic_slice_in_dim(offsets, first, wins_local, 0)
    mask = valid.astype(jnp.float32)
    weight = make_weight(nbins)
    window_specs = []
    for window in range(wins_local):
        series = records[window]
        cuts = jax.vmap(lambda start: lax.dynamic_slice_in_dim(series, start, SEGLEN, 1))(
            my_offsets[window]
        )
        spec = jnp.einsum("scn,qn->sqc", cuts, weight, preferred_element_type=jnp.float32)
        window_specs.append((spec * mask[window][None, None, :]).astype(jnp.bfloat16))
    local_spec = jnp.stack(window_specs, axis=0).reshape(wins_local * SEG * 2, nbins, chan_local)
    channels = chan_local * lax.axis_size("bins")
    row_count = channels // panels
    row_start = lax.axis_index("panel") * row_count
    scale = 1.0 / (wins_local * panels * SEG)
    per_bin = lax.all_to_all(local_spec, "bins", split_axis=1, concat_axis=2, tiled=True)
    whole = lax.all_gather(per_bin, "panel", axis=0, tiled=True)
    total = contract(whole, row_start, row_count)
    return (total * scale).astype(jnp.bfloat16)


def solution(mesh):
    placed = (P("panel", "bins", None), P("panel", "bins"), P())
    return jax.shard_map(
        body, mesh=mesh, in_specs=placed, out_specs=P("bins", "panel", None), check_vma=False
    )
```

profile of v0, /device:TPU:1, one launch (start us, length us, event | category | flops | bytes accessed | tf_op | source)
XLA Modules:
  0.0 312.3 jit_solution(15355156555567619553)
XLA Ops:
  8.4 3.8 %slice_bitcast_fusion.3 = (bf16[64,9216]{1,0:T(8,128)(2,1)}, bf16[64,9216]{1,0:T(8,128)(2,1)S(1)}, bf16[64,9216]{1,0:T(8,128)(2,1)S(1)}, bf16[64,9216]{1,0:T(8,128)(2,1)S(1)}) fusion(bf16[4,64,9216]{2,1,0:T(8,128)(2,1)} %param.3), kind=kLoop, calls=%fused_computation.25 | loop fusion | bytes 9437184 | tf_op jit(solution)/shard_map/squeeze | solution.py:49
  13.7 47.0 %while.4 = (s32[]{:T(128)}, bf16[64,9216]{1,0:T(8,128)(2,1)}, s32[16,2]{0,1:T(2,128)S(1)}, bf16[16,64,1024]{2,1,0:T(8,128)(2,1)}, s32[]{:T(128)}) while((s32[]{:T(128)}, bf16[64,9216]{1,0:T(8,128)(2,1)}, s32[16,2]{0,1:T(2,128)S(1)}, bf16[16,64,1024]{2,1,0:T(8,128)(2,1)}, s32[]{:T(128)}) %tuple.69), condition=%wide.while_cond, body=%wide.while_body.sunk | while | flops 2 | bytes 263257 | solution.py:50
  14.4 2.3 bitcast_dynamic-update-slice_fusion.8
  17.3 2.3 bitcast_dynamic-update-slice_fusion.8
  20.2 2.3 bitcast_dynamic-update-slice_fusion.8
  23.2 2.3 bitcast_dynamic-update-slice_fusion.8
  26.1 2.3 bitcast_dynamic-update-slice_fusion.8
  29.1 2.3 bitcast_dynamic-update-slice_fusion.8
  32.0 2.3 bitcast_dynamic-update-slice_fusion.8
  34.9 2.3 bitcast_dynamic-update-slice_fusion.8
  37.9 2.3 bitcast_dynamic-update-slice_fusion.8
  40.8 2.3 bitcast_dynamic-update-slice_fusion.8
  43.7 2.3 bitcast_dynamic-update-slice_fusion.8
  46.7 2.3 bitcast_dynamic-update-slice_fusion.8
  49.6 2.3 bitcast_dynamic-update-slice_fusion.8
  52.6 2.3 bitcast_dynamic-update-slice_fusion.8
  55.5 2.3 bitcast_dynamic-update-slice_fusion.8
  58.4 2.3 bitcast_dynamic-update-slice_fusion.8
  64.2 32.6 %while.6 = (s32[]{:T(128)}, bf16[64,9216]{1,0:T(8,128)(2,1)S(1)}, s32[16,2]{0,1:T(2,128)S(1)}, bf16[16,64,1024]{2,1,0:T(8,128)(2,1)}, s32[]{:T(128)}) while((s32[]{:T(128)}, bf16[64,9216]{1,0:T(8,128)(2,1)S(1)}, s32[16,2]{0,1:T(2,128)S(1)}, bf16[16,64,1024]{2,1,0:T(8,128)(2,1)}, s32[]{:T(128)}) %tuple.63), condition=%wide.while_cond.2, body=%wide.while_body.2.sunk | while | flops 2 | bytes 263257 | solution.py:50
  99.1 30.4 %while.5 = (s32[]{:T(128)}, bf16[64,9216]{1,0:T(8,128)(2,1)S(1)}, s32[16,2]{0,1:T(2,128)S(1)}, bf16[16,64,1024]{2,1,0:T(8,128)(2,1)}, s32[]{:T(128)}) while((s32[]{:T(128)}, bf16[64,9216]{1,0:T(8,128)(2,1)S(1)}, s32[16,2]{0,1:T(2,128)S(1)}, bf16[16,64,1024]{2,1,0:T(8,128)(2,1)}, s32[]{:T(128)}) %tuple.66), condition=%wide.while_cond.1, body=%wide.while_body.1.sunk | while | flops 2 | bytes 263257 | solution.py:50
  129.8 23.3 %while.7 = (s32[]{:T(128)}, bf16[64,9216]{1,0:T(8,128)(2,1)S(1)}, s32[16,2]{0,1:T(2,128)S(1)}, bf16[16,64,1024]{2,1,0:T(8,128)(2,1)S(1)}, s32[]{:T(128)}) while((s32[]{:T(128)}, bf16[64,9216]{1,0:T(8,128)(2,1)S(1)}, s32[16,2]{0,1:T(2,128)S(1)}, bf16[16,64,1024]{2,1,0:T(8,128)(2,1)S(1)}, s32[]{:T(128)}) %tuple.60), condition=%wide.while_cond.3, body=%wide.while_body.3.sunk | while | flops 2 | bytes 262241 | solution.py:50
  153.1 4.5 %fusion.10 = bf16[1,16,128,64]{2,3,1,0:T(8,128)(2,1)S(1)} fusion(bf16[16,64,1024]{2,1,0:T(8,128)(2,1)} %get-tuple-element.12, f32[64]{0:T(128)S(1)} %copy-done.7, s32[128]{0:T(128)S(1)} %copy-done.8, f32[1024]{0:T(1024)S(1)} %subtract_multiply_fusion, pred[128]{0:T(512)(128)(4,1)S(1)} %copy-done.9), kind=kOutput, calls=%fused_computation.29 | convolution fusion | flops 271056896 | bytes 2364288 | tf_op jit(solution)/shard_map/scn,qn->sqc/dot_general | solution.py:53
  157.7 2.8 fusion.8
  160.6 2.8 fusion.9
  163.4 2.8 fusion.7
  169.8 41.4 %all_to_all.12 = bf16[128,64,64]{0,2,1:T(8,128)(2,1)} all-to-all(bf16[128,64,64]{0,2,1:T(8,128)(2,1)S(1)} %copy.11), channel_id=1, replica_groups=mesh['bins'=64,'panel'=4] {'bins'}, dimensions={1} | all-to-all | bytes 2097152 | tf_op jit(solution)/shard_map/all_to_all | solution.py:60
  211.3 50.9 %all-gather.2.cloned.1.call-done = bf16[512,1,4096]{0,2,1:T(8,128)(2,1)} async-done(((bf16[128,1,4096]{0,2,1:T(8,128)(2,1)}), bf16[512,1,4096]{0,2,1:T(8,128)(2,1)}) %all-gather.2.cloned.1.call-update) | async-done | bytes 4194320 | tf_op jit(solution)/shard_map/all_gather | solution.py:61
  262.1 6.3 %copy.12 = bf16[512,1,4096]{2,0,1:T(8,128)(2,1)} copy(bf16[512,1,4096]{0,2,1:T(8,128)(2,1)} %all-gather.2.cloned.1.call-done) | data formatting | bytes 8388608 | tf_op jit(solution)/shard_map/all_gather | solution.py:61
  268.4 7.7 %reshape.198 = bf16[256,2,1,4096]{3,1,0,2:T(2,128)(2,1)} reshape(bf16[512,1,4096]{2,0,1:T(8,128)(2,1)} %copy.12) | data formatting | bytes 8388608 | tf_op jit(solution)/shard_map/reshape | solution.py:30
  276.1 7.6 %reshape.199 = bf16[256,2,4096]{2,1,0:T(2,128)(2,1)} reshape(bf16[512,1,4096]{2,0,1:T(8,128)(2,1)} %copy.12) | data formatting | bytes 8388608 | tf_op jit(solution)/shard_map/reshape.5
  283.7 4.1 %constant_dynamic-slice_fusion.5 = (bf16[256,1,1,1024]{3,1,0,2:T(2,128)(2,1)S(1)}, bf16[256,1,1,1024]{3,1,0,2:T(2,128)(2,1)S(1)}) fusion(bf16[256,2,1,4096]{3,1,0,2:T(2,128)(2,1)} %reshape.198, s32[]{:T(128)S(6)} %add.121, s32[]{:T(128)S(6)} %select_n.109), kind=kLoop, calls=%fused_computation.75 | loop fusion | bytes 2097160 | tf_op jit(solution)/shard_map/slice | solution.py:33
  290.0 15.5 %fusion.1 = bf16[1,1024,4096]{2,1,0:T(8,128)(2,1)} fusion(bf16[256,2,4096]{2,1,0:T(2,128)(2,1)} %reshape.199, bf16[256,1,1024]{0,2,1:T(8,128)(2,1)S(1)} %get-tuple-element.76, bf16[256,1,1024]{0,2,1:T(8,128)(2,1)S(1)} %get-tuple-element.75), kind=kOutput, calls=%fused_computation.10 | convolution fusion | flops 4303880192 | bytes 13631488 | tf_op jit(solution)/shard_map/kpfr,kpfc->frc/dot_general | solution.py:35
  (220 shorter events, 111.2 us)
Async XLA Ops:
  6.5 1.2 copy-start
  6.5 255.6 %all-gather.2.cloned.1.call-start = ((), (), s32[]{:S(2)}) async-start(), calls=%async_computation.1 | async-start | bytes 5242880 | tf_op jit(solution)/shard_map/all_gather | solution.py:61
  96.9 32.6 %copy-start.3 = (s32[16,1]{0,1:T(1,128)S(1)}, s32[16,1]{0,1:T(1,128)}, u32[]{:S(2)}) copy-start(s32[16,1]{0,1:T(1,128)} %get-tuple-element.82) | copy-start | bytes 196
  129.5 23.6 %copy-start.7 = (f32[64]{0:T(128)S(1)}, f32[64]{0:T(128)}, u32[]{:S(2)}) copy-start(f32[64]{0:T(128)} %get-tuple-element.77) | copy-start | bytes 772
  129.5 23.6 %copy-start.8 = (s32[128]{0:T(128)S(1)}, s32[128]{0:T(128)}, u32[]{:S(2)}) copy-start(s32[128]{0:T(128)} %fusion.45) | copy-start | bytes 1540
  129.5 23.6 %copy-start.9 = (pred[128]{0:T(512)(128)(4,1)S(1)}, pred[128]{0:T(512)(128)(4,1)}, u32[]{:S(2)}) copy-start(pred[128]{0:T(512)(128)(4,1)} %fusion.46) | copy-start | bytes 388
  153.1 4.6 %copy-start.1 = (bf16[16,64,1024]{2,1,0:T(8,128)(2,1)S(1)}, bf16[16,64,1024]{2,1,0:T(8,128)(2,1)}, u32[]{:S(2)}) copy-start(bf16[16,64,1024]{2,1,0:T(8,128)(2,1)} %get-tuple-element.28) | copy-start | bytes 6291460
  153.1 4.6 %copy-start.6 = (f32[64]{0:T(128)S(1)}, f32[64]{0:T(128)}, u32[]{:S(2)}) copy-start(f32[64]{0:T(128)} %get-tuple-element.79) | copy-start | bytes 772
  157.7 2.8 copy-start.2
  157.7 2.8 copy-start.5
  160.6 2.8 copy-start.4
Sparse Core Ops, SparseCore 0:
  211.4 50.7 all-gather.1
where the time goes:
time: 314 us; the launch traced here: 312 us
  local copies, waits for them, and re-layouts  175 us (56%)
  waiting for transfers between devices  50.9 us (16%)
  blocking collectives  41.4 us (13%)
  matrix products  28.5 us (9%)
  between operations  13.6 us (4%)
    gather x192, local copies, waits for them, and re-layouts  133 us
    all_gather x1, waiting for transfers between devices, body(): whole = lax.all_gather(per_bin, 'panel', axis=0, tiled=True)  50.9 us
    all_to_all x1, blocking collectives, body(): lax.all_to_all(local_spec, 'bins', split_axis=1, concat_axis=2, tiled=True)  41.4 us
    dot_general x1, matrix products, contract(): jnp.einsum('kpfr,kpfc->frc', left, halves, preferred_element_type=jnp.flo...  15.5 us
    dot_general x4, matrix products, body(): jnp.einsum('scn,qn->sqc', cuts, weight, preferred_element_type=jnp.float32)  13 us
    reshape x1, local copies, waits for them, and re-layouts, contract(): block.reshape(block.shape[0] // 2, 2, block.shape[1], block.shape[2])  7.66 us
    another operation x1, local copies, waits for them, and re-layouts  7.61 us
    unnamed x26, local copies, waits for them, and re-layouts  6.87 us
  transfers between devices with their start and end apart: 1, of which 1 were waited for; matrix products, arithmetic and copies ran while one was open for 0% of the time, Pallas kernels for 0%

commit v1 on v0

v1 whole, which is shorter than its diff:
```python
import functools

import jax
import jax.numpy as jnp
import numpy as np
from jax import lax
from jax.experimental import pallas as pl
from jax.experimental.pallas import tpu as pltpu
from jax.sharding import PartitionSpec as P

SEGLEN = 1024
SEG = 16
BAND0 = 64
MIB = 2**20


def weight_table(nbins):
    f32 = np.float32
    rows = np.arange(2 * nbins)
    freq = (BAND0 + rows % nbins)[:, None]
    pos = np.arange(SEGLEN)[None, :]
    hann = f32(0.5) - f32(0.5) * np.cos(f32(2.0 * np.pi) * pos.astype(f32) / f32(SEGLEN))
    taper = hann / np.sqrt(f32(0.375 * SEGLEN))
    phase = (freq * pos % SEGLEN).astype(f32) * f32(2.0 * np.pi / SEGLEN)
    trig = np.where((rows < nbins)[:, None], np.cos(phase), -np.sin(phase))
    return jnp.asarray((taper * trig).astype(jnp.bfloat16))


def cut(series, start):
    tile = jnp.minimum(start // 128, 63)
    inside = start - tile * 128
    base = pl.multiple_of(tile * 128, 128)
    keep = lax.broadcasted_iota(jnp.int32, (64, 128), 1) < 128 - inside
    shift = lax.rem(128 - inside, 128)
    turned = [pltpu.roll(series[:, pl.ds(base + 128 * t, 128)], shift, 1) for t in range(9)]
    return [jnp.where(keep, turned[t], turned[t + 1]) for t in range(8)]


def spectra_kernel(offsets, records, valid, weight, out, total):
    first = lax.axis_index("panel") * 4
    for low in range(2):
        high = low + 2
        mask = jnp.concatenate(
            [valid[pl.ds(low, 1), :].astype(jnp.float32), valid[pl.ds(high, 1), :].astype(jnp.float32)], axis=1
        )

        @pl.loop(0, SEG, unroll=4)
        def _(seg):
            cuts = jnp.concatenate(
                [
                    jnp.concatenate(cut(records.at[window], offsets[first + window, seg]), axis=1)
                    for window in (low, high)
                ],
                axis=0,
            )
            spec = lax.dot_general(weight[...], cuts, (((1,), (1,)), ((), ())), preferred_element_type=jnp.float32)
            spec = spec * mask
            for part in range(2):
                row = part * 32 + seg * 2 + low
                total[pl.ds(row, 64, stride=64), :] = spec[part * 64 : (part + 1) * 64]

    @pl.loop(0, 64, unroll=8)
    def _(k):
        out[k] = total[pl.ds(pl.multiple_of(k * 64, 64), 64), :].astype(jnp.bfloat16)


def spectra(records, valid, offsets):
    return pl.pallas_call(
        spectra_kernel,
        out_shape=jax.ShapeDtypeStruct((64, 64, 128), jnp.bfloat16),
        in_specs=[pl.BlockSpec(memory_space=pltpu.SMEM)] + [pl.BlockSpec(memory_space=pltpu.VMEM)] * 3,
        out_specs=pl.BlockSpec(memory_space=pltpu.VMEM),
        scratch_shapes=[pltpu.VMEM((4096, 128), jnp.float32)],
        compiler_params=pltpu.CompilerParams(vmem_limit_bytes=48 * MIB),
    )(offsets, records, valid, weight_table(64))


def pair_rows(even, odd):
    return jnp.concatenate(
        [
            jnp.concatenate([even[:, :64], odd[:, :64]], axis=1),
            jnp.concatenate([even[:, 64:], odd[:, 64:]], axis=1),
        ],
        axis=0,
    )


def left_rows(block):
    wide = block.astype(jnp.float32)
    rows = []
    for half in range(2):
        real_part = wide[half * 64 : half * 64 + 32]
        imag_part = wide[half * 64 + 32 : half * 64 + 64]
        rows += [real_part + imag_part, imag_part - real_part]
    return jnp.concatenate(rows, axis=0).T.astype(jnp.bfloat16)


def pack_kernel(whole, right, left):
    me = lax.axis_index("panel")

    @pl.loop(0, 32)
    def _(chip):
        column = pl.multiple_of(chip * 128, 128)
        for group in range(4):
            block = pair_rows(whole[group, 2 * chip], whole[group, 2 * chip + 1])
            right[group * 128 : (group + 1) * 128, pl.ds(column, 128)] = block

            @pl.when(chip // 8 == me)
            def _():
                row = pl.multiple_of(lax.rem(chip, 8) * 128, 128)
                left[pl.ds(row, 128), group * 128 : (group + 1) * 128] = left_rows(block)


def pack(whole):
    return pl.pallas_call(
        pack_kernel,
        out_shape=(
            jax.ShapeDtypeStruct((512, 4096), jnp.bfloat16),
            jax.ShapeDtypeStruct((1024, 512), jnp.bfloat16),
        ),
        in_specs=[pl.BlockSpec(memory_space=pltpu.VMEM)],
        out_specs=(pl.BlockSpec(memory_space=pltpu.VMEM),) * 2,
        compiler_params=pltpu.CompilerParams(vmem_limit_bytes=48 * MIB),
    )(whole)


def product_kernel(left, right, out):
    total = jnp.dot(left[...], right[...], preferred_element_type=jnp.float32)
    out[...] = (total * (1.0 / 256.0)).astype(jnp.bfloat16)


def product(left, right):
    width = 256
    return pl.pallas_call(
        product_kernel,
        grid=(4096 // width,),
        out_shape=jax.ShapeDtypeStruct((1024, 4096), jnp.bfloat16),
        in_specs=[
            pl.BlockSpec((1024, 512), lambda i: (0, 0)),
            pl.BlockSpec((512, width), lambda i: (0, i)),
        ],
        out_specs=pl.BlockSpec((1024, width), lambda i: (0, i)),
        compiler_params=pltpu.CompilerParams(vmem_limit_bytes=48 * MIB),
    )(left, right)


def body(records, valid, offsets):
    blocks = spectra(records, valid, offsets)
    per_bin = lax.all_to_all(blocks, "bins", split_axis=0, concat_axis=0, tiled=True)
    whole = lax.all_gather(per_bin, "panel", axis=0)
    right, left = pack(whole)
    return product(left, right)[None]


def solution(mesh):
    placed = (P("panel", "bins", None), P("panel", "bins"), P())
    return jax.shard_map(
        body, mesh=mesh, in_specs=placed, out_specs=P("bins", "panel", None), check_vma=False
    )
```

time: 314 us -> 140 us (0.45)
  local copies, waits for them, and re-layouts: 175 us -> 4.66 us
  Pallas kernels: 0 us -> 32.3 us
  matrix products: 28.5 us -> 0 us
    gather x192 -> x0, local copies, waits for them, and re-layouts: 133 us -> none
    pallas_call x0 -> x3, Pallas kernels: none -> 32.3 us  [the longest x1 15.2 us: pack(): pl.pallas_call(pack_kernel, out_shape=(jax.ShapeDtypeStruct((512, 4096),...]
    dot_general x5 -> x0, matrix products: 28.5 us -> none  [the longest x1 15.5 us: contract(): jnp.einsum('kpfr,kpfc->frc', left, halves, preferred_element_type=jnp.flo...]
    reshape x3 -> x0, local copies, waits for them, and re-layouts: 10.4 us -> none  [the longest x1 7.66 us: contract(): block.reshape(block.shape[0] // 2, 2, block.shape[1], block.shape[2])]
    another operation x2 -> x0, local copies, waits for them, and re-layouts: 8.3 us -> none
    all_gather x1 -> x0, local copies, waits for them, and re-layouts: 6.32 us -> none  [body(): whole = lax.all_gather(per_bin, 'panel', axis=0, tiled=True)]
    slice x1 -> x0, local copies, waits for them, and re-layouts: 4.13 us -> none  [contract(): imag_part = rows[:, 1].astype(jnp.float32)]
    squeeze x1 -> x0, local copies, waits for them, and re-layouts: 3.79 us -> none  [body(): series = records[window]]
where the time goes in v1:
time: 140 us
  waiting for transfers between devices  48 us (34%)
  blocking collectives  41.4 us (30%)
  Pallas kernels  32.3 us (23%)
  between operations  13.4 us (10%)
  local copies, waits for them, and re-layouts  4.66 us (3%)
    all_gather x1, waiting for transfers between devices, body(): whole = lax.all_gather(per_bin, 'panel', axis=0)  48 us
    all_to_all x1, blocking collectives, body(): lax.all_to_all(blocks, 'bins', split_axis=0, concat_axis=0, tiled=True)  41.4 us
    pallas_call x1, Pallas kernels, pack(): pl.pallas_call(pack_kernel, out_shape=(jax.ShapeDtypeStruct((512, 4096),...  15.2 us
    pallas_call x1, Pallas kernels, product(): pl.pallas_call(product_kernel, grid=(4096 // width,), out_shape=jax.Shape...  10.7 us
    pallas_call x1, Pallas kernels, spectra(): pl.pallas_call(spectra_kernel, out_shape=jax.ShapeDtypeStruct((64, 64, 12...  6.47 us
    unnamed x8, local copies, waits for them, and re-layouts  4.66 us
  transfers between devices with their start and end apart: 1, of which 1 were waited for; matrix products, arithmetic and copies ran while one was open for 0% of the time, Pallas kernels for 0%

profile of v1, /device:TPU:1, one launch (start us, length us, event | category | flops | bytes accessed | tf_op | source)
XLA Modules:
  0.0 139.9 jit_solution(13225154668114075856)
XLA Ops:
  6.5 0.0 all-gather.3.cloned.1.call-start
  6.5 0.0 copy-start
  6.5 2.3 %copy-done = bf16[4,64,9216]{2,1,0:T(8,128)(2,1)S(1)} copy-done((bf16[4,64,9216]{2,1,0:T(8,128)(2,1)S(1)}, bf16[4,64,9216]{2,1,0:T(8,128)(2,1)}, u32[]{:S(2)}) %copy-start) | copy-done | bytes 4718616
  8.9 0.0 copy-start.1
  8.9 0.9 copy-done.1
  9.8 0.0 copy-start.2
  9.8 0.7 copy-done.2
  10.5 0.0 copy-start.3
  10.5 0.7 copy-done.3
  11.2 6.5 %shard_map.46 = bf16[64,64,128]{2,1,0:T(8,128)(2,1)S(1)} custom-call(s32[16,16]{1,0:T(8,128)S(1)} %copy-done.2, bf16[4,64,9216]{2,1,0:T(8,128)(2,1)S(1)} %copy-done, s32[4,64]{1,0:T(4,128)S(1)} %copy-done.3, bf16[128,1024]{1,0:T(8,128)(2,1)S(1)} %copy-done.1), custom_call_target="tpu_custom_call" | custom-call | tf_op jit(solution)/shard_map/pallas_call | solution.py:68
  17.7 41.4 %all_to_all.5 = bf16[64,64,128]{2,1,0:T(8,128)(2,1)} all-to-all(bf16[64,64,128]{2,1,0:T(8,128)(2,1)S(1)} %shard_map.46), channel_id=1, replica_groups=mesh['bins'=64,'panel'=4] {'bins'}, dimensions={0} | all-to-all | bytes 2097152 | tf_op jit(solution)/shard_map/all_to_all | solution.py:149
  59.1 0.0 all-gather.3.cloned.1.call-update
  59.1 48.0 %all-gather.3.cloned.1.call-done = bf16[256,64,128]{2,1,0:T(8,128)(2,1)} async-done(((bf16[64,64,128]{2,1,0:T(8,128)(2,1)}), bf16[256,64,128]{2,1,0:T(8,128)(2,1)}) %all-gather.3.cloned.1.call-update) | async-done | bytes 4194320 | tf_op jit(solution)/shard_map/all_gather | solution.py:150
  107.2 15.2 %shard_map.47 = (bf16[512,4096]{1,0:T(8,128)(2,1)S(1)}, bf16[1024,512]{1,0:T(8,128)(2,1)S(1)}) custom-call(bf16[4,64,64,128]{3,2,1,0:T(8,128)(2,1)} %bitcast.2), custom_call_target="tpu_custom_call" | custom-call | tf_op jit(solution)/shard_map/pallas_call | solution.py:115
  122.4 10.7 %shard_map.48 = bf16[1024,4096]{1,0:T(8,128)(2,1)} custom-call(bf16[1024,512]{1,0:T(8,128)(2,1)S(1)} %get-tuple-element.7.left, bf16[512,4096]{1,0:T(8,128)(2,1)S(1)} %get-tuple-element.8.right), custom_call_target="tpu_custom_call" | custom-call | tf_op jit(solution)/shard_map/pallas_call | solution.py:134
Async XLA Ops:
  6.5 100.6 %all-gather.3.cloned.1.call-start = ((), (), s32[]{:S(2)}) async-start(), calls=%async_computation.1 | async-start | bytes 5242880 | tf_op jit(solution)/shard_map/all_gather | solution.py:150
  6.5 2.3 %copy-start = (bf16[4,64,9216]{2,1,0:T(8,128)(2,1)S(1)}, bf16[4,64,9216]{2,1,0:T(8,128)(2,1)}, u32[]{:S(2)}) copy-start(bf16[4,64,9216]{2,1,0:T(8,128)(2,1)} %records.1) | copy-start | bytes 14155780
  8.9 0.9 copy-start.1
  9.8 0.7 copy-start.2
  10.5 0.7 copy-start.3
Sparse Core Ops, SparseCore 0:
  59.3 47.8 all-gather.2

commit v2 on v1

v2 whole, which is shorter than its diff:
```python
import functools

import jax
import jax.numpy as jnp
import numpy as np
from jax import lax
from jax.experimental import pallas as pl
from jax.experimental.pallas import tpu as pltpu
from jax.sharding import PartitionSpec as P

SEGLEN = 1024
SEG = 16
BAND0 = 64
MIB = 2**20
SCALE = 1.0 / 256.0
MESH = pl.DeviceIdType.MESH


def weight_table(nbins):
    f32 = np.float32
    rows = np.arange(2 * nbins)
    freq = (BAND0 + rows % nbins)[:, None]
    pos = np.arange(SEGLEN)[None, :]
    hann = f32(0.5) - f32(0.5) * np.cos(f32(2.0 * np.pi) * pos.astype(f32) / f32(SEGLEN))
    taper = hann / np.sqrt(f32(0.375 * SEGLEN))
    phase = (freq * pos % SEGLEN).astype(f32) * f32(2.0 * np.pi / SEGLEN)
    trig = np.where((rows < nbins)[:, None], np.cos(phase), -np.sin(phase))
    return jnp.asarray((taper * trig).astype(jnp.bfloat16))


def cut(series, start):
    tile = jnp.minimum(start // 128, 63)
    inside = start - tile * 128
    base = pl.multiple_of(tile * 128, 128)
    keep = lax.broadcasted_iota(jnp.int32, (64, 128), 1) < 128 - inside
    shift = lax.rem(128 - inside, 128)
    turned = [pltpu.roll(series[:, pl.ds(base + 128 * t, 128)], shift, 1) for t in range(9)]
    return [jnp.where(keep, turned[t], turned[t + 1]) for t in range(8)]


XSTEP = (0, 1, 3, 2)
ZSTEP = (0, 4, 1, 7, 3, 5, 2, 6)
STEPS = [(dx, dz) for dx in XSTEP for dz in ZSTEP]
RELAY_LAG = 6
PRODUCT_LAG = 10


def pair_rows(even, odd):
    return jnp.concatenate(
        [
            jnp.concatenate([even[:, :64], odd[:, :64]], axis=1),
            jnp.concatenate([even[:, 64:], odd[:, 64:]], axis=1),
        ],
        axis=0,
    )


def left_rows(block):
    wide = block.astype(jnp.float32)
    rows = []
    for at in range(0, 128, 32):
        real_part = wide[at : at + 16]
        imag_part = wide[at + 16 : at + 32]
        rows += [real_part + imag_part, imag_part - real_part]
    return jnp.concatenate(rows, axis=0).T.astype(jnp.bfloat16)


def spectra_kernel(offsets_in, records, valid, weight, blocks, offsets, series, mask_in, table, total, in_sems):
    me = lax.axis_index("panel")
    loads = [
        pltpu.make_async_copy(offsets_in, offsets, in_sems.at[6]),
        pltpu.make_async_copy(valid, mask_in, in_sems.at[4]),
        pltpu.make_async_copy(weight, table, in_sems.at[5]),
    ]
    reads = [pltpu.make_async_copy(records.at[w], series[w], in_sems.at[w]) for w in range(4)]
    for copy in (*loads, reads[0], reads[2], reads[1], reads[3]):
        copy.start()
    for copy in loads:
        copy.wait()

    for low in range(2):
        reads[low].wait()
        reads[low + 2].wait()
        mask = jnp.concatenate(
            [mask_in[w : w + 1, :].astype(jnp.float32) for w in (low, low + 2)], axis=1
        )

        @pl.loop(0, SEG, unroll=4)
        def _(seg):
            cuts = jnp.concatenate(
                [
                    jnp.concatenate(cut(series[w], offsets[me * 4 + w, seg]), axis=1)
                    for w in (low, low + 2)
                ],
                axis=0,
            )
            spec = lax.dot_general(table[...], cuts, (((1,), (1,)), ((), ())), preferred_element_type=jnp.float32)
            spec = spec * mask
            for part in range(2):
                row = low * 32 + part * 16 + seg
                total[pl.ds(row, 64, stride=64), :] = spec[part * 64 : (part + 1) * 64]

    @pl.loop(0, 64, unroll=8)
    def _(k):
        blocks[k] = total[pl.ds(pl.multiple_of(k * 64, 64), 64), :].astype(jnp.bfloat16)


def spectra(records, valid, offsets):
    bf16 = jnp.bfloat16
    return pl.pallas_call(
        spectra_kernel,
        out_shape=pltpu.VMEM((64, 64, 128), bf16),
        in_specs=[pl.BlockSpec(memory_space=pltpu.HBM)] * 4,
        out_specs=pl.BlockSpec(memory_space=pltpu.VMEM),
        scratch_shapes=[
            pltpu.SMEM((16, 16), jnp.int32),
            [pltpu.VMEM((64, 9216), bf16) for _ in range(4)],
            pltpu.VMEM((4, 64), jnp.int32),
            pltpu.VMEM((128, SEGLEN), bf16),
            pltpu.VMEM((4096, 128), jnp.float32),
            pltpu.SemaphoreType.DMA((7,)),
        ],
        compiler_params=pltpu.CompilerParams(vmem_limit_bytes=36 * MIB),
    )(*(pltpu.with_memory_space_constraint(a, pltpu.HBM) for a in (offsets, records, valid, weight_table(64))))


def main_kernel(
    blocks, right, left, whole,
    own_sem, plane_send, plane_recv, ring_send, ring_recv, relay_send, relay_recv,
):
    b = lax.axis_index("bins")
    me = lax.axis_index("panel")
    x, z, core = b // 16, lax.rem(b // 2, 8), lax.rem(b, 2)
    chip = b // 2
    up, down, across = lax.rem(me + 1, 4), lax.rem(me + 3, 4), lax.rem(me + 2, 4)

    barrier = pltpu.get_barrier_semaphore()

    @pl.loop(1, 64)
    def _(i):
        pl.semaphore_signal(barrier, inc=1, device_id={"bins": lax.rem(b + i, 64)}, device_id_type=MESH)

    for there in (up, down):
        pl.semaphore_signal(barrier, inc=1, device_id={"panel": there}, device_id_type=MESH)

    pl.semaphore_wait(barrier, 65)

    own = pltpu.make_async_copy(blocks.at[b], whole.at[me, b], own_sem)
    own.start()

    def send(dx, dz, there_core):
        there = (lax.rem(x + dx, 4) * 8 + lax.rem(z + dz, 8)) * 2 + there_core
        pltpu.make_async_remote_copy(
            blocks.at[there], whole.at[me, b], plane_send, plane_recv.at[chip],
            device_id={"bins": there}, device_id_type=MESH,
        ).start()

    for dx, dz in STEPS:
        if (dx, dz) != (0, 0):
            send(dx, dz, core)
        send(dx, dz, 1 - core)
    own.wait()

    def source(step):
        dx, dz = STEPS[step]
        return lax.rem(x + 4 - dx, 4) * 8 + lax.rem(z + 8 - dz, 8)

    def chunk(group, k, there, send_sem, recv_sem):
        part = whole.at[group, pl.ds(2 * k, 2)]
        return pltpu.make_async_remote_copy(
            part, part, send_sem, recv_sem, device_id={"panel": there}, device_id_type=MESH
        )

    def plane_arrival(step):
        n = 2 if step else 1
        part = blocks.at[pl.ds(0, n)]
        pltpu.make_async_remote_copy(
            part, part, plane_send, plane_recv.at[source(step)], device_id={"bins": b}, device_id_type=MESH
        ).wait_recv()

    def forward(step):
        k = source(step)
        chunk(me, k, up, ring_send, ring_recv.at[0, k]).start()
        chunk(me, k, down, ring_send, ring_recv.at[1, k]).start()

    def relay(step):
        k = source(step)
        chunk(down, k, up, ring_send, ring_recv.at[0, k]).wait_recv()
        chunk(up, k, down, ring_send, ring_recv.at[1, k]).wait_recv()
        if step % 2 == 0:
            chunk(down, k, up, relay_send, relay_recv.at[k]).start()
        else:
            chunk(up, k, down, relay_send, relay_recv.at[k]).start()

    def use(step):
        k = source(step)
        chunk(across, k, up, relay_send, relay_recv.at[k]).wait_recv()
        column = pl.ds(pl.multiple_of(k * 128, 128), 128)
        for group in range(4):
            rows = slice(group * 128, (group + 1) * 128)
            block = pair_rows(whole[group, 2 * k], whole[group, 2 * k + 1])
            right[rows, column] = block

        @pl.when(k // 8 == me)
        def _():
            place = pl.ds(pl.multiple_of(lax.rem(k, 8) * 128, 128), 128)
            for group in range(4):
                rows = slice(group * 128, (group + 1) * 128)
                left[place, rows] = left_rows(right[rows, column])

    last = len(STEPS)
    for step in range(last + PRODUCT_LAG):
        if step < last:
            plane_arrival(step)
            forward(step)
        if 0 <= step - RELAY_LAG < last:
            relay(step - RELAY_LAG)
        if step >= PRODUCT_LAG:
            use(step - PRODUCT_LAG)

    def sent(part, sem):
        pltpu.make_async_remote_copy(
            part, part, sem, relay_recv.at[0], device_id={"panel": up}, device_id_type=MESH
        ).wait_send()

    sent(blocks.at[pl.ds(0, 63)], plane_send)
    sent(whole.at[pl.ds(0, 2)], ring_send)
    sent(whole.at[0], relay_send)


def main(blocks):
    dma = pltpu.SemaphoreType.DMA
    bf16 = jnp.bfloat16
    return pl.pallas_call(
        main_kernel,
        out_shape=(pltpu.VMEM((512, 4096), bf16), pltpu.VMEM((1024, 512), bf16)),
        in_specs=[pl.BlockSpec(memory_space=pltpu.VMEM)],
        out_specs=(pl.BlockSpec(memory_space=pltpu.VMEM),) * 2,
        scratch_shapes=[
            pltpu.VMEM((4, 64, 64, 128), bf16),
            dma(()), dma(()), dma((32,)), dma(()), dma((2, 32)), dma(()), dma((32,)),
        ],
        compiler_params=pltpu.CompilerParams(
            collective_id=0, has_side_effects=True, vmem_limit_bytes=36 * MIB
        ),
        cost_estimate=pl.CostEstimate(flops=10**10, bytes_accessed=2 * 10**7, transcendentals=0),
    )(pltpu.with_memory_space_constraint(blocks, pltpu.VMEM))


def product_kernel(right, left, out, result, sems):
    copies = []
    for at in range(8):
        wide = pl.ds(at * 512, 512)
        part = jnp.dot(left[...], right[:, wide], preferred_element_type=jnp.float32)
        result[:, wide] = (part * SCALE).astype(jnp.bfloat16)
        copies.append(pltpu.make_async_copy(result.at[:, wide], out.at[:, wide], sems.at[at]))
        copies[-1].start()
    for copy in copies:
        copy.wait()


def product(right, left):
    return pl.pallas_call(
        product_kernel,
        out_shape=jax.ShapeDtypeStruct((1024, 4096), jnp.bfloat16),
        in_specs=[pl.BlockSpec(memory_space=pltpu.VMEM)] * 2,
        out_specs=pl.BlockSpec(memory_space=pl.ANY),
        scratch_shapes=[pltpu.VMEM((1024, 4096), jnp.bfloat16), pltpu.SemaphoreType.DMA((8,))],
        compiler_params=pltpu.CompilerParams(vmem_limit_bytes=36 * MIB),
    )(*(pltpu.with_memory_space_constraint(a, pltpu.VMEM) for a in (right, left)))


def body(records, valid, offsets):
    return product(*main(spectra(records, valid, offsets)))[None]


def solution(mesh):
    placed = (P("panel", "bins", None), P("panel", "bins"), P())
    return jax.shard_map(
        body, mesh=mesh, in_specs=placed, out_specs=P("bins", "panel", None), check_vma=False
    )
```

time: 140 us -> 67.5 us (0.48)
  waiting for transfers between devices: 48 us -> 0 us
  blocking collectives: 41.4 us -> 0 us
  Pallas kernels: 32.3 us -> 67.4 us
  between operations: 13.4 us -> 0.02 us
  local copies, waits for them, and re-layouts: 4.66 us -> 0 us
    all_gather x1 -> x0, waiting for transfers between devices: 48 us -> none  [body(): whole = lax.all_gather(per_bin, 'panel', axis=0)]
    all_to_all x1 -> x0, blocking collectives: 41.4 us -> none  [body(): lax.all_to_all(blocks, 'bins', split_axis=0, concat_axis=0, tiled=True)]
    pallas_call x3, Pallas kernels: 32.3 us -> 67.4 us  [the longest x1 54.2 us: main(): pl.pallas_call(main_kernel, out_shape=(pltpu.VMEM((512, 4096), bf16), plt...]
    unnamed x8 -> x0, local copies, waits for them, and re-layouts: 4.66 us -> none
  transfers between devices with their start and end apart: 1 -> 0, of which waited for: 1 -> 0; matrix products, arithmetic and copies ran while one was open for 0% -> 0% of each run, Pallas kernels for 0% -> 0%
where the time goes in v2:
time: 67.5 us; the launch traced here: 67.4 us
  Pallas kernels  67.4 us (100%)
    pallas_call x1, Pallas kernels, main(): pl.pallas_call(main_kernel, out_shape=(pltpu.VMEM((512, 4096), bf16), plt...  54.2 us
    pallas_call x1, Pallas kernels, spectra(): pl.pallas_call(spectra_kernel, out_shape=pltpu.VMEM((64, 64, 128), bf16),...  7.56 us
    pallas_call x1, Pallas kernels, product(): pl.pallas_call(product_kernel, out_shape=jax.ShapeDtypeStruct((1024, 4096...  5.56 us

profile of v2, /device:TPU:1, one launch (start us, length us, event | category | flops | bytes accessed | tf_op | source)
XLA Modules:
  0.0 67.4 jit_solution(1984173667723633661)
XLA Ops:
  0.0 7.6 %shard_map.46.blocks = bf16[64,64,128]{2,1,0:T(8,128)(2,1)S(1)} custom-call(s32[16,16]{1,0:T(8,128)} %offsets_in.1, bf16[4,64,9216]{2,1,0:T(8,128)(2,1)} %records.1, s32[4,64]{1,0:T(4,128)} %valid.1, bf16[128,1024]{1,0:T(8,128)(2,1)} %constant.2.clone.weight), custom_call_target="tpu_custom_call" | custom-call | tf_op jit(solution)/shard_map/pallas_call | solution.py:110
  7.6 54.2 %shard_map.47 = (bf16[512,4096]{1,0:T(8,128)(2,1)S(1)}, bf16[1024,512]{1,0:T(8,128)(2,1)S(1)}) custom-call(bf16[64,64,128]{2,1,0:T(8,128)(2,1)S(1)} %shard_map.46.blocks), custom_call_target="tpu_custom_call" | custom-call | flops 10000000000 | bytes 20000000 | tf_op jit(solution)/shard_map/pallas_call | solution.py:234
  61.8 5.6 %shard_map.48 = bf16[1024,4096]{1,0:T(8,128)(2,1)} custom-call(bf16[512,4096]{1,0:T(8,128)(2,1)S(1)} %get-tuple-element.7.right, bf16[1024,512]{1,0:T(8,128)(2,1)S(1)} %get-tuple-element.8.left), custom_call_target="tpu_custom_call" | custom-call | tf_op jit(solution)/shard_map/pallas_call | solution.py:263

commit v3 on v2

--- a/solution.py
+++ b/solution.py
@@ -39,10 +39,11 @@
 
 
 XSTEP = (0, 1, 3, 2)
-ZSTEP = (0, 4, 1, 7, 3, 5, 2, 6)
+ZSTEP = (0, 1, 7, 2, 6, 3, 5, 4)
 STEPS = [(dx, dz) for dx in XSTEP for dz in ZSTEP]
 RELAY_LAG = 6
 PRODUCT_LAG = 10
+EARLY = 8
 
 
 def pair_rows(even, odd):
@@ -65,67 +66,69 @@
     return jnp.concatenate(rows, axis=0).T.astype(jnp.bfloat16)
 
 
-def spectra_kernel(offsets_in, records, valid, weight, blocks, offsets, series, mask_in, table, total, in_sems):
+def cuts_kernel(offsets_in, records, valid, weight, cuts, table, mask, offsets, series, mask_in, in_sems):
     me = lax.axis_index("panel")
-    loads = [
-        pltpu.make_async_copy(offsets_in, offsets, in_sems.at[6]),
-        pltpu.make_async_copy(valid, mask_in, in_sems.at[4]),
-        pltpu.make_async_copy(weight, table, in_sems.at[5]),
+    load = pltpu.make_async_copy(offsets_in, offsets, in_sems.at[8])
+    load.start()
+    reads = []
+    for part, (first, count) in enumerate(((0, 5248), (5248, 3968))):
+        for low in range(2):
+            for w in (low, low + 2):
+                place = pl.ds(first, count)
+                reads.append(
+                    pltpu.make_async_copy(records.at[w, :, place], series[w].at[:, place], in_sems.at[part * 4 + w])
+                )
+    others = [
+        pltpu.make_async_copy(valid, mask_in, in_sems.at[9]),
+        pltpu.make_async_copy(weight, table, in_sems.at[10]),
     ]
-    reads = [pltpu.make_async_copy(records.at[w], series[w], in_sems.at[w]) for w in range(4)]
-    for copy in (*loads, reads[0], reads[2], reads[1], reads[3]):
+    for copy in (*reads, *others):
         copy.start()
-    for copy in loads:
+    load.wait()
+    for part in range(2):
+        for low in range(2):
+            for copy in reads[part * 4 + low * 2 : part * 4 + low * 2 + 2]:
+                copy.wait()
+
+            @pl.loop(part * 8, part * 8 + 8, unroll=4)
+            def _(seg):
+                for half in range(2):
+                    w = low + 2 * half
+                    tiles = cut(series[w], offsets[me * 4 + w, seg])
+                    for t in range(8):
+                        cuts[low * SEG + seg, half * 64 : half * 64 + 64, t * 128 : t * 128 + 128] = tiles[t]
+
+    for copy in others:
         copy.wait()
-
     for low in range(2):
-        reads[low].wait()
-        reads[low + 2].wait()
-        mask = jnp.concatenate(
+        mask[low : low + 1, :] = jnp.concatenate(
             [mask_in[w : w + 1, :].astype(jnp.float32) for w in (low, low + 2)], axis=1
         )
 
-        @pl.loop(0, SEG, unroll=4)
-        def _(seg):
-            cuts = jnp.concatenate(
-                [
-                    jnp.concatenate(cut(series[w], offsets[me * 4 + w, seg]), axis=1)
-                    for w in (low, low + 2)
-                ],
-                axis=0,
-            )
-            spec = lax.dot_general(table[...], cuts, (((1,), (1,)), ((), ())), preferred_element_type=jnp.float32)
-            spec = spec * mask
-            for part in range(2):
-                row = low * 32 + part * 16 + seg
-                total[pl.ds(row, 64, stride=64), :] = spec[part * 64 : (part + 1) * 64]
-
-    @pl.loop(0, 64, unroll=8)
-    def _(k):
-        blocks[k] = total[pl.ds(pl.multiple_of(k * 64, 64), 64), :].astype(jnp.bfloat16)
-
-
-def spectra(records, valid, offsets):
+
+def segments(records, valid, offsets):
     bf16 = jnp.bfloat16
     return pl.pallas_call(
-        spectra_kernel,
-        out_shape=pltpu.VMEM((64, 64, 128), bf16),
+        cuts_kernel,
+        out_shape=(
+            pltpu.VMEM((2 * SEG, 128, SEGLEN), bf16),
+            pltpu.VMEM((128, SEGLEN), bf16),
+            pltpu.VMEM((2, 128), jnp.float32),
+        ),
         in_specs=[pl.BlockSpec(memory_space=pltpu.HBM)] * 4,
-        out_specs=pl.BlockSpec(memory_space=pltpu.VMEM),
+        out_specs=(pl.BlockSpec(memory_space=pltpu.VMEM),) * 3,
         scratch_shapes=[
             pltpu.SMEM((16, 16), jnp.int32),
             [pltpu.VMEM((64, 9216), bf16) for _ in range(4)],
             pltpu.VMEM((4, 64), jnp.int32),
-            pltpu.VMEM((128, SEGLEN), bf16),
-            pltpu.VMEM((4096, 128), jnp.float32),
-            pltpu.SemaphoreType.DMA((7,)),
+            pltpu.SemaphoreType.DMA((11,)),
         ],
-        compiler_params=pltpu.CompilerParams(vmem_limit_bytes=36 * MIB),
+        compiler_params=pltpu.CompilerParams(vmem_limit_bytes=32 * MIB),
     )(*(pltpu.with_memory_space_constraint(a, pltpu.HBM) for a in (offsets, records, valid, weight_table(64))))
 
 
 def main_kernel(
-    blocks, right, left, whole,
+    cuts, table, mask, right, left, total, blocks, whole,
     own_sem, plane_send, plane_recv, ring_send, ring_recv, relay_send, relay_recv,
 ):
     b = lax.axis_index("bins")
@@ -143,22 +146,43 @@
     for there in (up, down):
         pl.semaphore_signal(barrier, inc=1, device_id={"panel": there}, device_id_type=MESH)
 
+    def spectra(low):
+        keep = mask[low : low + 1, :]
+
+        @pl.loop(0, SEG, unroll=4)
+        def _(seg):
+            spec = lax.dot_general(
+                table[...], cuts[low * SEG + seg], (((1,), (1,)), ((), ())), preferred_element_type=jnp.float32
+            )
+            spec = spec * keep
+            for part in range(2):
+                total[pl.ds(part * 16 + seg, 64, stride=32), :] = spec[part * 64 : (part + 1) * 64]
+
+        @pl.loop(0, 64, unroll=8)
+        def _(k):
+            blocks[k, low * 32 : low * 32 + 32] = total[pl.ds(pl.multiple_of(k * 32, 32), 32), :].astype(jnp.bfloat16)
+
+    def send(step, first, count):
+        dx, dz = STEPS[step]
+        rows = pl.ds(first, count)
+        for there_core in (core, 1 - core) if step else (1 - core,):
+            there = (lax.rem(x + dx, 4) * 8 + lax.rem(z + dz, 8)) * 2 + there_core
+            pltpu.make_async_remote_copy(
+                blocks.at[there, rows], whole.at[me, b, rows], plane_send, plane_recv.at[chip],
+                device_id={"bins": there}, device_id_type=MESH,
+            ).start()
+
+    spectra(0)
     pl.semaphore_wait(barrier, 65)
-
+    for step in range(EARLY):
+        send(step, 0, 32)
+    spectra(1)
     own = pltpu.make_async_copy(blocks.at[b], whole.at[me, b], own_sem)
     own.start()
-
-    def send(dx, dz, there_core):
-        there = (lax.rem(x + dx, 4) * 8 + lax.rem(z + dz, 8)) * 2 + there_core
-        pltpu.make_async_remote_copy(
-            blocks.at[there], whole.at[me, b], plane_send, plane_recv.at[chip],
-            device_id={"bins": there}, device_id_type=MESH,
-        ).start()
-
-    for dx, dz in STEPS:
-        if (dx, dz) != (0, 0):
-            send(dx, dz, core)
-        send(dx, dz, 1 - core)
+    for step in range(EARLY):
+        send(step, 32, 32)
+    for step in range(EARLY, len(STEPS)):
+        send(step, 0, 64)
     own.wait()
 
     def source(step):
@@ -228,23 +252,25 @@
     sent(whole.at[0], relay_send)
 
 
-def main(blocks):
+def main(cuts, table, mask):
     dma = pltpu.SemaphoreType.DMA
     bf16 = jnp.bfloat16
     return pl.pallas_call(
         main_kernel,
         out_shape=(pltpu.VMEM((512, 4096), bf16), pltpu.VMEM((1024, 512), bf16)),
-        in_specs=[pl.BlockSpec(memory_space=pltpu.VMEM)],
+        in_specs=[pl.BlockSpec(memory_space=pltpu.VMEM)] * 3,
         out_specs=(pl.BlockSpec(memory_space=pltpu.VMEM),) * 2,
         scratch_shapes=[
+            pltpu.VMEM((64 * 32, 128), jnp.float32),
+            pltpu.VMEM((64, 64, 128), bf16),
             pltpu.VMEM((4, 64, 64, 128), bf16),
             dma(()), dma(()), dma((32,)), dma(()), dma((2, 32)), dma(()), dma((32,)),
         ],
         compiler_params=pltpu.CompilerParams(
-            collective_id=0, has_side_effects=True, vmem_limit_bytes=36 * MIB
+            collective_id=0, has_side_effects=True, vmem_limit_bytes=32 * MIB
         ),
         cost_estimate=pl.CostEstimate(flops=10**10, bytes_accessed=2 * 10**7, transcendentals=0),
-    )(pltpu.with_memory_space_constraint(blocks, pltpu.VMEM))
+    )(*(pltpu.with_memory_space_constraint(a, pltpu.VMEM) for a in (cuts, table, mask)))
 
 
 def product_kernel(right, left, out, result, sems):
@@ -266,12 +292,12 @@
         in_specs=[pl.BlockSpec(memory_space=pltpu.VMEM)] * 2,
         out_specs=pl.BlockSpec(memory_space=pl.ANY),
         scratch_shapes=[pltpu.VMEM((1024, 4096), jnp.bfloat16), pltpu.SemaphoreType.DMA((8,))],
-        compiler_params=pltpu.CompilerParams(vmem_limit_bytes=36 * MIB),
+        compiler_params=pltpu.CompilerParams(vmem_limit_bytes=32 * MIB),
     )(*(pltpu.with_memory_space_constraint(a, pltpu.VMEM) for a in (right, left)))
 
 
 def body(records, valid, offsets):
-    return product(*main(spectra(records, valid, offsets)))[None]
+    return product(*main(*segments(records, valid, offsets)))[None]
 
 
 def solution(mesh):

time: 67.5 us -> 65.3 us (0.967)
  Pallas kernels: 67.4 us -> 64.8 us
    pallas_call x1, Pallas kernels: 7.56 us -> 4.56 us  [segments(): pl.pallas_call(cuts_kernel, out_shape=(pltpu.VMEM((2 * SEG, 128, SEGLEN),...]
where the time goes in v3:
time: 65.3 us; the launch traced here: 64.9 us
  Pallas kernels  64.8 us (99%)
    pallas_call x1, Pallas kernels, main(): pl.pallas_call(main_kernel, out_shape=(pltpu.VMEM((512, 4096), bf16), plt...  54.7 us
    pallas_call x1, Pallas kernels, product(): pl.pallas_call(product_kernel, out_shape=jax.ShapeDtypeStruct((1024, 4096...  5.56 us
    pallas_call x1, Pallas kernels, segments(): pl.pallas_call(cuts_kernel, out_shape=(pltpu.VMEM((2 * SEG, 128, SEGLEN),...  4.56 us

profile of v3, /device:TPU:1, one launch (start us, length us, event | category | flops | bytes accessed | tf_op | source)
XLA Modules:
  0.0 64.9 jit_solution(8382408186222530281)
XLA Ops:
  0.0 4.6 %shard_map.46 = (bf16[32,128,1024]{2,1,0:T(8,128)(2,1)S(1)}, bf16[128,1024]{1,0:T(8,128)(2,1)S(1)}, f32[2,128]{1,0:T(2,128)S(1)}) custom-call(s32[16,16]{1,0:T(8,128)} %offsets_in.1, bf16[4,64,9216]{2,1,0:T(8,128)(2,1)} %records.1, s32[4,64]{1,0:T(4,128)} %valid.1, bf16[128,1024]{1,0:T(8,128)(2,1)} %constant.2.clone.weight), custom_call_target="tpu_custom_call" | custom-call | tf_op jit(solution)/shard_map/pallas_call | solution.py:111
  4.6 54.7 %shard_map.47 = (bf16[512,4096]{1,0:T(8,128)(2,1)S(1)}, bf16[1024,512]{1,0:T(8,128)(2,1)S(1)}) custom-call(bf16[32,128,1024]{2,1,0:T(8,128)(2,1)S(1)} %get-tuple-element.10.cuts, bf16[128,1024]{1,0:T(8,128)(2,1)S(1)} %get-tuple-element.11.table, f32[2,128]{1,0:T(2,128)S(1)} %get-tuple-element.12.mask), custom_call_target="tpu_custom_call" | custom-call | flops 10000000000 | bytes 20000000 | tf_op jit(solution)/shard_map/pallas_call | solution.py:258
  59.3 5.6 %shard_map.48 = bf16[1024,4096]{1,0:T(8,128)(2,1)} custom-call(bf16[512,4096]{1,0:T(8,128)(2,1)S(1)} %get-tuple-element.13.right, bf16[1024,512]{1,0:T(8,128)(2,1)S(1)} %get-tuple-element.14.left), custom_call_target="tpu_custom_call" | custom-call | tf_op jit(solution)/shard_map/pallas_call | solution.py:289

commit v4 on v3

--- a/solution.py
+++ b/solution.py
@@ -128,7 +128,7 @@
 
 
 def main_kernel(
-    cuts, table, mask, right, left, total, blocks, whole,
+    cuts, table, mask, right, left, early, total, blocks, whole,
     own_sem, plane_send, plane_recv, ring_send, ring_recv, relay_send, relay_recv,
 ):
     b = lax.axis_index("bins")
@@ -225,12 +225,21 @@
             block = pair_rows(whole[group, 2 * k], whole[group, 2 * k + 1])
             right[rows, column] = block
 
+        turned = (2 - STEPS[step][1]) % 8 * 128
+
         @pl.when(k // 8 == me)
         def _():
-            place = pl.ds(pl.multiple_of(lax.rem(k, 8) * 128, 128), 128)
             for group in range(4):
                 rows = slice(group * 128, (group + 1) * 128)
-                left[place, rows] = left_rows(right[rows, column])
+                left[turned : turned + 128, rows] = left_rows(right[rows, column])
+
+    def multiply_early(slab):
+        first = lax.rem(x + 4 - XSTEP[slab], 4) * 1024
+        for half in range(2):
+            wide = pl.ds(pl.multiple_of(first + half * 512, 512), 512)
+            part = jnp.dot(left[:512, :], right[:, wide], preferred_element_type=jnp.float32)
+            place = slab * 1024 + half * 512
+            early[:, place : place + 512] = (part * SCALE).astype(jnp.bfloat16)
 
     last = len(STEPS)
     for step in range(last + PRODUCT_LAG):
@@ -241,6 +250,8 @@
             relay(step - RELAY_LAG)
         if step >= PRODUCT_LAG:
             use(step - PRODUCT_LAG)
+            if 0 <= step - PRODUCT_LAG - 27 < 3:
+                multiply_early(step - PRODUCT_LAG - 27)
 
     def sent(part, sem):
         pltpu.make_async_remote_copy(
@@ -257,9 +268,13 @@
     bf16 = jnp.bfloat16
     return pl.pallas_call(
         main_kernel,
-        out_shape=(pltpu.VMEM((512, 4096), bf16), pltpu.VMEM((1024, 512), bf16)),
+        out_shape=(
+            pltpu.VMEM((512, 4096), bf16),
+            pltpu.VMEM((1024, 512), bf16),
+            pltpu.VMEM((512, 3072), bf16),
+        ),
         in_specs=[pl.BlockSpec(memory_space=pltpu.VMEM)] * 3,
-        out_specs=(pl.BlockSpec(memory_space=pltpu.VMEM),) * 2,
+        out_specs=(pl.BlockSpec(memory_space=pltpu.VMEM),) * 3,
         scratch_shapes=[
             pltpu.VMEM((64 * 32, 128), jnp.float32),
             pltpu.VMEM((64, 64, 128), bf16),
@@ -273,27 +288,51 @@
     )(*(pltpu.with_memory_space_constraint(a, pltpu.VMEM) for a in (cuts, table, mask)))
 
 
-def product_kernel(right, left, out, result, sems):
+def product_kernel(right, left, early, out, result, sems):
+    b = lax.axis_index("bins")
+    x, z = b // 16, lax.rem(b // 2, 8)
     copies = []
-    for at in range(8):
-        wide = pl.ds(at * 512, 512)
-        part = jnp.dot(left[...], right[:, wide], preferred_element_type=jnp.float32)
-        result[:, wide] = (part * SCALE).astype(jnp.bfloat16)
-        copies.append(pltpu.make_async_copy(result.at[:, wide], out.at[:, wide], sems.at[at]))
-        copies[-1].start()
+
+    def store(held, slab, half):
+        first = pl.multiple_of(lax.rem(x + 4 - XSTEP[slab], 4) * 1024, 1024)
+        for at in range(half * 4, half * 4 + 4):
+            row = pl.multiple_of(lax.rem(z + 6 + at, 8) * 128, 128)
+            copies.append(
+                pltpu.make_async_copy(
+                    held.at[pl.ds(at * 128, 128), pl.ds(slab * 1024, 1024)],
+                    out.at[pl.ds(row, 128), pl.ds(first, 1024)],
+                    sems.at[slab, at],
+                )
+            )
+            copies[-1].start()
+
+    def multiply(slab, half):
+        first = lax.rem(x + 4 - XSTEP[slab], 4) * 1024
+        rows = pl.ds(half * 512, 512)
+        for at in range(2):
+            wide = pl.ds(pl.multiple_of(first + at * 512, 512), 512)
+            part = jnp.dot(left[rows, :], right[:, wide], preferred_element_type=jnp.float32)
+            result[rows, pl.ds(slab * 1024 + at * 512, 512)] = (part * SCALE).astype(jnp.bfloat16)
+        store(result, slab, half)
+
+    for slab in range(3):
+        store(early, slab, 0)
+    multiply(3, 0)
+    for slab in range(4):
+        multiply(slab, 1)
     for copy in copies:
         copy.wait()
 
 
-def product(right, left):
+def product(right, left, early):
     return pl.pallas_call(
         product_kernel,
         out_shape=jax.ShapeDtypeStruct((1024, 4096), jnp.bfloat16),
-        in_specs=[pl.BlockSpec(memory_space=pltpu.VMEM)] * 2,
+        in_specs=[pl.BlockSpec(memory_space=pltpu.VMEM)] * 3,
         out_specs=pl.BlockSpec(memory_space=pl.ANY),
-        scratch_shapes=[pltpu.VMEM((1024, 4096), jnp.bfloat16), pltpu.SemaphoreType.DMA((8,))],
+        scratch_shapes=[pltpu.VMEM((1024, 4096), jnp.bfloat16), pltpu.SemaphoreType.DMA((4, 8))],
         compiler_params=pltpu.CompilerParams(vmem_limit_bytes=32 * MIB),
-    )(*(pltpu.with_memory_space_constraint(a, pltpu.VMEM) for a in (right, left)))
+    )(*(pltpu.with_memory_space_constraint(a, pltpu.VMEM) for a in (right, left, early)))
 
 
 def body(records, valid, offsets):

time: 65.3 us -> 64.9 us (level)
    pallas_call x1, Pallas kernels: 5.56 us -> 4.22 us  [product(): pl.pallas_call(product_kernel, out_shape=jax.ShapeDtypeStruct((1024, 4096...]
    pallas_call x1, Pallas kernels: 54.7 us -> 56 us  [main(): pl.pallas_call(main_kernel, out_shape=(pltpu.VMEM((512, 4096), bf16), plt...]
where the time goes in v4:
time: 64.9 us; the launch traced here: 64.8 us
  Pallas kernels  64.8 us (100%)
    pallas_call x1, Pallas kernels, main(): pl.pallas_call(main_kernel, out_shape=(pltpu.VMEM((512, 4096), bf16), plt...  56 us
    pallas_call x1, Pallas kernels, segments(): pl.pallas_call(cuts_kernel, out_shape=(pltpu.VMEM((2 * SEG, 128, SEGLEN),...  4.56 us
    pallas_call x1, Pallas kernels, product(): pl.pallas_call(product_kernel, out_shape=jax.ShapeDtypeStruct((1024, 4096...  4.22 us

profile of v4, /device:TPU:1, one launch (start us, length us, event | category | flops | bytes accessed | tf_op | source)
XLA Modules:
  0.0 64.8 jit_solution(6144606915829455085)
XLA Ops:
  0.0 4.6 %shard_map.46 = (bf16[32,128,1024]{2,1,0:T(8,128)(2,1)S(1)}, bf16[128,1024]{1,0:T(8,128)(2,1)S(1)}, f32[2,128]{1,0:T(2,128)S(1)}) custom-call(s32[16,16]{1,0:T(8,128)} %offsets_in.1, bf16[4,64,9216]{2,1,0:T(8,128)(2,1)} %records.1, s32[4,64]{1,0:T(4,128)} %valid.1, bf16[128,1024]{1,0:T(8,128)(2,1)} %constant.2.clone.weight), custom_call_target="tpu_custom_call" | custom-call | tf_op jit(solution)/shard_map/pallas_call | solution.py:111
  4.6 56.0 %shard_map.47 = (bf16[512,4096]{1,0:T(8,128)(2,1)S(1)}, bf16[1024,512]{1,0:T(8,128)(2,1)S(1)}, bf16[512,3072]{1,0:T(8,128)(2,1)S(1)}) custom-call(bf16[32,128,1024]{2,1,0:T(8,128)(2,1)S(1)} %get-tuple-element.11.cuts, bf16[128,1024]{1,0:T(8,128)(2,1)S(1)} %get-tuple-element.12.table, f32[2,128]{1,0:T(2,128)S(1)} %get-tuple-element.13.mask), custom_call_target="tpu_custom_call" | custom-call | flops 10000000000 | bytes 20000000 | tf_op jit(solution)/shard_map/pallas_call | solution.py:269
  60.6 4.2 %shard_map.48 = bf16[1024,4096]{1,0:T(8,128)(2,1)} custom-call(bf16[512,4096]{1,0:T(8,128)(2,1)S(1)} %get-tuple-element.14.right, bf16[1024,512]{1,0:T(8,128)(2,1)S(1)} %get-tuple-element.15.left, bf16[512,3072]{1,0:T(8,128)(2,1)S(1)} %get-tuple-element.16.early), custom_call_target="tpu_custom_call" | custom-call | tf_op jit(solution)/shard_map/pallas_call | solution.py:328

commit v5 on v4

--- a/solution.py
+++ b/solution.py
@@ -44,6 +44,7 @@
 RELAY_LAG = 6
 PRODUCT_LAG = 10
 EARLY = 8
+DIRECT = (8, 16, 24)
 
 
 def pair_rows(even, odd):
@@ -146,6 +147,16 @@
     for there in (up, down):
         pl.semaphore_signal(barrier, inc=1, device_id={"panel": there}, device_id_type=MESH)
 
+    def target(step, there_core):
+        dx, dz = STEPS[step]
+        return (lax.rem(x + dx, 4) * 8 + lax.rem(z + dz, 8)) * 2 + there_core
+
+    for step in DIRECT:
+        for there_core in range(2):
+            for there in (up, down):
+                place = {"bins": target(step, there_core), "panel": there}
+                pl.semaphore_signal(barrier, inc=1, device_id=place, device_id_type=MESH)
+
     def spectra(low):
         keep = mask[low : low + 1, :]
 
@@ -163,22 +174,34 @@
             blocks[k, low * 32 : low * 32 + 32] = total[pl.ds(pl.multiple_of(k * 32, 32), 32), :].astype(jnp.bfloat16)
 
     def send(step, first, count):
-        dx, dz = STEPS[step]
         rows = pl.ds(first, count)
         for there_core in (core, 1 - core) if step else (1 - core,):
-            there = (lax.rem(x + dx, 4) * 8 + lax.rem(z + dz, 8)) * 2 + there_core
+            there = target(step, there_core)
             pltpu.make_async_remote_copy(
                 blocks.at[there, rows], whole.at[me, b, rows], plane_send, plane_recv.at[chip],
                 device_id={"bins": there}, device_id_type=MESH,
             ).start()
 
+    def send_direct(first, count):
+        rows = pl.ds(first, count)
+        for step in DIRECT:
+            for there_core in (core, 1 - core):
+                there = target(step, there_core)
+                for way, panel in ((0, up), (1, down)):
+                    pltpu.make_async_remote_copy(
+                        blocks.at[there, rows], whole.at[me, b, rows], ring_send, ring_recv.at[way, chip],
+                        device_id={"bins": there, "panel": panel}, device_id_type=MESH,
+                    ).start()
+
     spectra(0)
-    pl.semaphore_wait(barrier, 65)
+    pl.semaphore_wait(barrier, 65 + 4 * len(DIRECT))
+    send_direct(0, 32)
     for step in range(EARLY):
         send(step, 0, 32)
     spectra(1)
     own = pltpu.make_async_copy(blocks.at[b], whole.at[me, b], own_sem)
     own.start()
+    send_direct(32, 32)
     for step in range(EARLY):
         send(step, 32, 32)
     for step in range(EARLY, len(STEPS)):
@@ -245,7 +268,8 @@
     for step in range(last + PRODUCT_LAG):
         if step < last:
             plane_arrival(step)
-            forward(step)
+            if step not in DIRECT:
+                forward(step)
         if 0 <= step - RELAY_LAG < last:
             relay(step - RELAY_LAG)
         if step >= PRODUCT_LAG:

time: 64.9 us -> 62.2 us (0.958)
  Pallas kernels: 64.8 us -> 62.1 us
    pallas_call x1, Pallas kernels: 56 us -> 53.3 us  [main(): pl.pallas_call(main_kernel, out_shape=(pltpu.VMEM((512, 4096), bf16), plt...]
where the time goes in v5:
time: 62.2 us; the launch traced here: 62.1 us
  Pallas kernels  62.1 us (100%)
    pallas_call x1, Pallas kernels, main(): pl.pallas_call(main_kernel, out_shape=(pltpu.VMEM((512, 4096), bf16), plt...  53.3 us
    pallas_call x1, Pallas kernels, segments(): pl.pallas_call(cuts_kernel, out_shape=(pltpu.VMEM((2 * SEG, 128, SEGLEN),...  4.56 us
    pallas_call x1, Pallas kernels, product(): pl.pallas_call(product_kernel, out_shape=jax.ShapeDtypeStruct((1024, 4096...  4.22 us

profile of v5, /device:TPU:1, one launch (start us, length us, event | category | flops | bytes accessed | tf_op | source)
XLA Modules:
  0.0 62.1 jit_solution(5225895223517035884)
XLA Ops:
  0.0 4.6 %shard_map.46 = (bf16[32,128,1024]{2,1,0:T(8,128)(2,1)S(1)}, bf16[128,1024]{1,0:T(8,128)(2,1)S(1)}, f32[2,128]{1,0:T(2,128)S(1)}) custom-call(s32[16,16]{1,0:T(8,128)} %offsets_in.1, bf16[4,64,9216]{2,1,0:T(8,128)(2,1)} %records.1, s32[4,64]{1,0:T(4,128)} %valid.1, bf16[128,1024]{1,0:T(8,128)(2,1)} %constant.2.clone.weight), custom_call_target="tpu_custom_call" | custom-call | tf_op jit(solution)/shard_map/pallas_call | solution.py:112
  4.6 53.3 %shard_map.47 = (bf16[512,4096]{1,0:T(8,128)(2,1)S(1)}, bf16[1024,512]{1,0:T(8,128)(2,1)S(1)}, bf16[512,3072]{1,0:T(8,128)(2,1)S(1)}) custom-call(bf16[32,128,1024]{2,1,0:T(8,128)(2,1)S(1)} %get-tuple-element.11.cuts, bf16[128,1024]{1,0:T(8,128)(2,1)S(1)} %get-tuple-element.12.table, f32[2,128]{1,0:T(2,128)S(1)} %get-tuple-element.13.mask), custom_call_target="tpu_custom_call" | custom-call | flops 10000000000 | bytes 20000000 | tf_op jit(solution)/shard_map/pallas_call | solution.py:293
  57.9 4.2 %shard_map.48 = bf16[1024,4096]{1,0:T(8,128)(2,1)} custom-call(bf16[512,4096]{1,0:T(8,128)(2,1)S(1)} %get-tuple-element.14.right, bf16[1024,512]{1,0:T(8,128)(2,1)S(1)} %get-tuple-element.15.left, bf16[512,3072]{1,0:T(8,128)(2,1)S(1)} %get-tuple-element.16.early), custom_call_target="tpu_custom_call" | custom-call | tf_op jit(solution)/shard_map/pallas_call | solution.py:352

commit v6 on v5

--- a/solution.py
+++ b/solution.py
@@ -43,7 +43,7 @@
 STEPS = [(dx, dz) for dx in XSTEP for dz in ZSTEP]
 RELAY_LAG = 6
 PRODUCT_LAG = 10
-EARLY = 8
+EARLY = 4
 DIRECT = (8, 16, 24)
 
 
@@ -91,7 +91,7 @@
             for copy in reads[part * 4 + low * 2 : part * 4 + low * 2 + 2]:
                 copy.wait()
 
-            @pl.loop(part * 8, part * 8 + 8, unroll=4)
+            @pl.loop(part * 8, part * 8 + 8, unroll=8)
             def _(seg):
                 for half in range(2):
                     w = low + 2 * half

time: 62.2 us -> 63.2 us (1.016)
  Pallas kernels: 62.1 us -> 62.9 us
    pallas_call x1, Pallas kernels: 53.3 us -> 54.4 us  [main(): pl.pallas_call(main_kernel, out_shape=(pltpu.VMEM((512, 4096), bf16), plt...]
where the time goes in v6:
time: 63.2 us; the launch traced here: 63 us
  Pallas kernels  62.9 us (100%)
    pallas_call x1, Pallas kernels, main(): pl.pallas_call(main_kernel, out_shape=(pltpu.VMEM((512, 4096), bf16), plt...  54.4 us
    pallas_call x1, Pallas kernels, product(): pl.pallas_call(product_kernel, out_shape=jax.ShapeDtypeStruct((1024, 4096...  4.22 us
    pallas_call x1, Pallas kernels, segments(): pl.pallas_call(cuts_kernel, out_shape=(pltpu.VMEM((2 * SEG, 128, SEGLEN),...  4.21 us

profile of v6, /device:TPU:1, one launch (start us, length us, event | category | flops | bytes accessed | tf_op | source)
XLA Modules:
  0.0 63.0 jit_solution(3362240619799168338)
XLA Ops:
  0.0 4.2 %shard_map.46 = (bf16[32,128,1024]{2,1,0:T(8,128)(2,1)S(1)}, bf16[128,1024]{1,0:T(8,128)(2,1)S(1)}, f32[2,128]{1,0:T(2,128)S(1)}) custom-call(s32[16,16]{1,0:T(8,128)} %offsets_in.1, bf16[4,64,9216]{2,1,0:T(8,128)(2,1)} %records.1, s32[4,64]{1,0:T(4,128)} %valid.1, bf16[128,1024]{1,0:T(8,128)(2,1)} %constant.2.clone.weight), custom_call_target="tpu_custom_call" | custom-call | tf_op jit(solution)/shard_map/pallas_call | solution.py:112
  4.2 54.4 %shard_map.47 = (bf16[512,4096]{1,0:T(8,128)(2,1)S(1)}, bf16[1024,512]{1,0:T(8,128)(2,1)S(1)}, bf16[512,3072]{1,0:T(8,128)(2,1)S(1)}) custom-call(bf16[32,128,1024]{2,1,0:T(8,128)(2,1)S(1)} %get-tuple-element.11.cuts, bf16[128,1024]{1,0:T(8,128)(2,1)S(1)} %get-tuple-element.12.table, f32[2,128]{1,0:T(2,128)S(1)} %get-tuple-element.13.mask), custom_call_target="tpu_custom_call" | custom-call | flops 10000000000 | bytes 20000000 | tf_op jit(solution)/shard_map/pallas_call | solution.py:293
  58.7 4.2 %shard_map.48 = bf16[1024,4096]{1,0:T(8,128)(2,1)} custom-call(bf16[512,4096]{1,0:T(8,128)(2,1)S(1)} %get-tuple-element.14.right, bf16[1024,512]{1,0:T(8,128)(2,1)S(1)} %get-tuple-element.15.left, bf16[512,3072]{1,0:T(8,128)(2,1)S(1)} %get-tuple-element.16.early), custom_call_target="tpu_custom_call" | custom-call | tf_op jit(solution)/shard_map/pallas_call | solution.py:352
